TPU v7x, 512 devices: a whole 4x4x16 slice. The times are simulated.
512 devices in a mesh: lat: 16 (over z_lo, core), lon: 32 (over z_hi, x, y).
Axes of the slice: x: 4, y: 4, z: 16 (z_hi: 2, z_lo: 8; z = z_hi * 8 + z_lo), core: 2. Of those that a mesh axis runs over, the one named last changes fastest.
Arguments:
- tokens: bfloat16 [1, 192, 384, 512], P(None, 'lat', 'lon'), may hold values from -8 to 8
- gain_first: float32 [512], replicated, may hold values from 0.1 to 1.9
- qkv_first: bfloat16 [512, 1536], replicated, may hold values from -16 to 16
- proj_first: bfloat16 [512, 512], replicated, may hold values from -0.25 to 0.25
- bias_first: float32 [16, 16, 529], P('lat'), may hold values from -6 to 6
- gain_second: float32 [512], replicated, may hold values from 0.1 to 1.9
- qkv_second: bfloat16 [512, 1536], replicated, may hold values from -16 to 16
- proj_second: bfloat16 [512, 512], replicated, may hold values from -0.25 to 0.25
- bias_second: float32 [16, 16, 529], P('lat'), may hold values from -6 to 6
Outputs:
- mixed: bfloat16 [1, 192, 384, 512], P(None, 'lat', 'lon')
All inputs are finite; a program needn't handle non-finite values.
Results may differ from a plain program's by a relative error of at most 0.012.
The roundings to bfloat16 on the way count: a program that leaves them out, or rounds other values in their place, can miss the bound.
Values may be sent and summed in bfloat16 or wider, within the bound.
A program may use at most 64 MiB of HBM per device.

v0:
```python
import jax
import jax.numpy as jnp
from jax import lax
from jax.sharding import PartitionSpec as P

HEADS = 16
LEV = 1
WH = 12
WW = 12


def shifted(block, axis, distance):
    devices = range(lax.axis_size(axis))
    route = [((i - distance) % len(devices), i) for i in devices]
    return lax.ppermute(block, axis, route)


def offsets():
    count = LEV * WH * WW
    index = jnp.arange(count, dtype=jnp.int32)
    level = index // (WH * WW)
    row = index // WW % WH
    column = index % WW
    first = level[:, None] - level[None, :] + LEV - 1
    second = row[:, None] - row[None, :] + WH - 1
    third = column[:, None] - column[None, :] + WW - 1
    return (first * (2 * WH - 1) + second) * (2 * WW - 1) + third


def to_windows(tile):
    levels, rows, cols, width = tile.shape
    shaped = tile.reshape(levels, rows, cols // WW, WW, width)
    return shaped.transpose(2, 0, 1, 3, 4).reshape(cols // WW, levels * rows * WW, width)


def from_windows(wins, cols):
    width = wins.shape[-1]
    shaped = wins.reshape(cols // WW, LEV, WH, WW, width)
    return shaped.transpose(1, 2, 0, 3, 4).reshape(LEV, WH, cols, width)


def norm_rows(values, gain):
    data = values.astype(jnp.float32)
    mean = jnp.mean(data, axis=-1, keepdims=True)
    centred = data - mean
    var = jnp.mean(centred * centred, axis=-1, keepdims=True)
    return (centred * lax.rsqrt(var + 1e-05) * gain).astype(jnp.bfloat16)


def project_all(normed, wqkv):
    width = normed.shape[-1]
    flat = jnp.dot(normed.reshape(-1, width), wqkv, preferred_element_type=jnp.float32)
    return flat.reshape(normed.shape[:-1] + (3 * width,))


def attend_split(query, keys, values, wproj, bias, allowed):
    count, size, width = query.shape
    head_dim = width // HEADS
    query = query.reshape(count, size, HEADS, head_dim)
    keys = keys.reshape(count, size, HEADS, head_dim)
    values = values.reshape(count, size, HEADS, head_dim)
    scores = jnp.einsum("wqhd,wkhd->whqk", query, keys, precision=lax.Precision.HIGHEST)
    scores = scores * head_dim ** (-0.5) + bias[None]
    if allowed is not None:
        scores = jnp.where(allowed[None, None], scores, -1e30)
    top = jnp.max(scores, axis=-1, keepdims=True)
    expo = jnp.exp(scores - top)
    weights = (expo / jnp.sum(expo, axis=-1, keepdims=True)).astype(jnp.bfloat16)
    heads_out = jnp.einsum("whqk,wkhd->wqhd", weights, values, preferred_element_type=jnp.float32)
    heads_out = heads_out.reshape(count * size, width).astype(jnp.bfloat16)
    return jnp.dot(heads_out, wproj, preferred_element_type=jnp.float32).reshape(count, size, width)


def attend_tokens(wins, gain, wqkv, wproj, bias, allowed):
    width = wins.shape[-1]
    mixed = project_all(norm_rows(wins, gain), wqkv)
    query = mixed[..., :width]
    keys = mixed[..., width : 2 * width]
    values = mixed[..., 2 * width :].astype(jnp.bfloat16)
    return attend_split(query, keys, values, wproj, bias, allowed)


def shards(
    tokens,
    gain_first,
    qkv_first,
    proj_first,
    bias_first,
    gain_second,
    qkv_second,
    proj_second,
    bias_second,
):
    levels, rows, cols, width = tokens.shape
    rel = offsets()
    count = LEV * WH * WW
    half_rows = WH // 2
    half_cols = WW // 2
    wins = to_windows(tokens)
    bias_one = jnp.take(bias_first[0], rel, axis=1)
    result = wins.astype(jnp.float32) + attend_tokens(
        wins, gain_first, qkv_first, proj_first, bias_one, None
    )
    first = from_windows(result.astype(jnp.bfloat16), cols)
    index = jnp.arange(count, dtype=jnp.int32)
    lower = index // WW % WH >= half_rows
    polar = lax.axis_index("lat") == lax.axis_size("lat") - 1
    group = jnp.logical_and(lower, polar)
    allowed = group[:, None] == group[None, :]
    bias_two = jnp.take(bias_second[0], rel, axis=1)
    east = shifted(first[:, :, :half_cols], "lon", -1)
    shifted_cols = jnp.concatenate([first[:, :, half_cols:], east], axis=2)
    south = shifted(shifted_cols[:, :half_rows], "lat", -1)
    window = to_windows(jnp.concatenate([shifted_cols[:, half_rows:], south], axis=1))
    branch = window.astype(jnp.float32) + attend_tokens(
        window, gain_second, qkv_second, proj_second, bias_two, allowed
    )
    back = from_windows(branch.astype(jnp.bfloat16), cols)
    north = shifted(back[:, half_rows:], "lat", 1)
    rows_back = jnp.concatenate([north, back[:, :half_rows]], axis=1)
    west = shifted(rows_back[:, :, cols - half_cols :], "lon", 1)
    mixed_out = jnp.concatenate([west, rows_back[:, :, : cols - half_cols]], axis=2)
    return mixed_out


def solution(mesh):
    placed = (
        P(None, "lat", "lon", None),
        P(),
        P(),
        P(),
        P("lat", None, None),
        P(),
        P(),
        P(),
        P("lat", None, None),
    )
    return jax.shard_map(
        shards, mesh=mesh, in_specs=placed, out_specs=P(None, "lat", "lon", None), check_vma=False
    )
```

profile of v0, /device:TPU:1, one launch (start us, length us, event | category | flops | bytes accessed | tf_op | source)
XLA Modules:
  0.0 206.1 jit_solution(13218745037913778471)
XLA Ops:
  0.0 0.0 copy-start
  0.0 1.1 reshape.438
  1.1 1.0 reshape.439
  2.0 1.0 convert_reduce_fusion
  3.1 0.1 div.75
  3.2 0.2 multiply_reduce_fusion
  3.4 0.0 copy-done
  3.4 0.0 copy-start.9
  3.5 1.1 convolution_bitcast_fusion.1
  4.6 0.8 fusion.25
  5.4 0.1 compare_select_fusion
  5.5 0.2 compare_and_fusion
  5.7 0.9 copy.20
  6.5 0.0 copy-done.9
  6.5 0.1 copy.24
  6.7 0.1 reshape.462
  6.9 38.7 %gather_fusion = f32[20736,16]{1,0:T(8,128)} fusion(f32[16,529]{0,1:T(8,128)S(1)} %bitcast.52, s32[21504]{0:T(1024)S(1)} %pad_clamp_fusion), kind=kCustom, calls=%fused_computation.clone | custom fusion | bytes 2737152 | tf_op jit(solution)/shard_map/jit(_take)/gather | solution.py:100
  45.5 12.2 %copy.26 = f32[144,144,16]{0,1,2:T(8,128)} copy(f32[144,144,16]{2,1,0:T(8,128)} %bitcast.55) | data formatting | bytes 2654208 | tf_op jit(solution)/shard_map/jit(_take)/gather | solution.py:100
  57.7 0.2 copy.21
  57.9 1.2 copy.22
  59.1 0.1 copy.23
  59.2 4.1 %bitcast_add_fusion.1 = f32[16,144,144]{1,2,0:T(8,128)S(1)} fusion(f32[144,144,16]{0,1,2:T(8,128)} %copy.26, f32[144,16,32]{0,2,1:T(8,128)S(1)} %bitcast.56, f32[144,16,32]{0,2,1:T(8,128)S(1)} %bitcast.58, pred[144,144]{0,1:T(8,128)(4,1)S(1)} %copy.23), kind=kOutput, calls=%fused_computation.8 | convolution fusion | flops 128397312 | bytes 3264768 | tf_op jit(solution)/shard_map/wqhd,wkhd->whqk/dot_general | solution.py:62
  63.3 0.0 copy-start.2
  63.3 1.4 copy-done.2
  64.7 0.5 fusion.28
  65.2 0.5 copy-done.7
  65.7 3.1 %convolution_convert_fusion.1 = bf16[16,32,144]{2,1,0:T(8,128)(2,1)S(1)} fusion(bf16[144,16,32]{0,2,1:T(8,128)(2,1)S(1)} %bitcast.62, f32[16,144]{1,0:T(8,128)S(1)} %fusion.28, f32[16,144,144]{1,2,0:T(8,128)} %copy-done.2), kind=kOutput, calls=%fused_computation.14 | convolution fusion | flops 22305168 | bytes 1631232 | tf_op jit(solution)/shard_map/whqk,wkhd->wqhd/dot_general | solution.py:69
  68.8 0.0 copy-start.10
  68.8 0.0 copy-done.5
  68.8 0.3 fusion.3
  69.1 0.1 reshape_transpose_reshape.10
  69.2 0.3 fusion.26
  69.5 20.9 %collective-permute-start = (bf16[1,12,6,512]{3,0,2,1:T(2,128)(2,1)S(1)}, bf16[1,12,6,512]{3,0,2,1:T(2,128)(2,1)S(1)}, u32[]{:S(2)}, u32[]{:S(2)}) collective-permute-start(bf16[1,12,6,512]{3,0,2,1:T(2,128)(2,1)S(1)} %get-tuple-element.16), channel_id=1, source_target_pairs={{1,0},{2,1},{3,2},{4,3},{5,4},{6,5},{7,6},{8,7},{9,8},{10,9},{11,1... | collective-permute-start | bytes 221192 | tf_op jit(solution)/shard_map/ppermute | solution.py:15
  90.4 12.5 %collective-permute-done = bf16[1,12,6,512]{3,0,2,1:T(2,128)(2,1)S(1)} collective-permute-done((bf16[1,12,6,512]{3,0,2,1:T(2,128)(2,1)S(1)}, bf16[1,12,6,512]{3,0,2,1:T(2,128)(2,1)S(1)}, u32[]{:S(2)}, u32[]{:S(2)}) %collective-permute-start) | collective-permute-done | bytes 73760 | tf_op jit(solution)/shard_map/ppermute | solution.py:15
  103.0 1.1 fusion.8
  104.1 2.6 %collective-permute-start.1 = (bf16[1,6,12,512]{3,0,2,1:T(2,128)(2,1)}, bf16[1,6,12,512]{3,0,2,1:T(2,128)(2,1)}, u32[]{:S(2)}, u32[]{:S(2)}) collective-permute-start(bf16[1,6,12,512]{3,0,2,1:T(2,128)(2,1)} %get-tuple-element.14), channel_id=1, source_target_pairs={{32,0},{64,32},{96,64},{128,96},{160,128},{192,160},{224,192},{256... | collective-permute-start | bytes 221192 | tf_op jit(solution)/shard_map/ppermute | solution.py:15
  106.6 0.1 broadcast_compare_fusion
  106.7 0.0 copy-done.10
  106.8 0.1 copy.34
  106.9 38.7 %gather_fusion.1 = f32[20736,16]{1,0:T(8,128)} fusion(f32[16,529]{0,1:T(8,128)S(1)} %bitcast.53, s32[21504]{0:T(1024)S(1)} %pad_clamp_fusion), kind=kCustom, calls=%fused_computation.1.clone | custom fusion | bytes 2737152 | tf_op jit(solution)/shard_map/jit(_take)/gather | solution.py:110
  145.6 12.2 %copy.36 = f32[144,144,16]{0,1,2:T(8,128)} copy(f32[144,144,16]{2,1,0:T(8,128)} %bitcast.54) | data formatting | bytes 2654208 | tf_op jit(solution)/shard_map/jit(_take)/gather | solution.py:110
  157.8 0.0 collective-permute-done.1
  157.8 0.0 copy-done.4
  157.8 3.6 %fusion.23 = (f32[12,12]{1,0:T(8,128)S(1)}, f32[12,12,512]{2,1,0:T(8,128)}, f32[1,12,12,512]{3,0,2,1:T(1,128)}) fusion(bf16[1,6,12,512]{3,0,2,1:T(2,128)(2,1)} %collective-permute-done.1, bf16[1,6,12,512]{3,0,2,1:T(2,128)(2,1)S(1)} %copy-done.4), kind=kLoop, calls=%fused_computation.68 | loop fusion | flops 221040 | bytes 737856 | tf_op jit(solution)/shard_map/reduce_sum | solution.py:44
  161.4 1.0 reshape.440
  162.4 0.1 div.82
  162.5 2.9 %fusion.6 = f32[144]{0:T(256)S(1)} fusion(f32[1,12,12,512]{3,0,2,1:T(1,128)} %get-tuple-element.8, f32[144]{0:T(256)S(1)} %div.82), kind=kLoop, calls=%fused_computation.30 | loop fusion | flops 221040 | bytes 296064 | tf_op jit(solution)/shard_map/reduce_sum | solution.py:46
  165.4 0.0 copy-done.11
  165.4 0.4 convolution_bitcast_fusion
  166.0 0.8 copy.30
  166.8 0.2 copy.31
  167.0 0.2 copy.32
  167.2 4.3 %fusion.2 = f32[16,144,144]{1,2,0:T(8,128)S(1)} fusion(f32[144,144,16]{0,1,2:T(8,128)} %copy.36, f32[144,16,32]{0,2,1:T(8,128)S(1)} %bitcast.57, f32[144,16,32]{0,2,1:T(8,128)S(1)} %bitcast.59, pred[144,144]{0,1:T(8,128)(4,1)S(1)} %copy.23, pred[144,144]{0,1:T(8,128)(4,1)S(1)} %broadcast_compare_fusion), kind=kOutput, calls=%fused_computation.7 | convolution fusion | flops 128729088 | bytes 3285504 | tf_op jit(solution)/shard_map/wqhd,wkhd->whqk/dot_general | solution.py:62
  171.5 1.4 copy-done.1
  172.9 0.5 fusion.29
  173.4 0.5 copy-done.8
  173.9 3.1 %convolution_convert_fusion = bf16[16,32,144]{2,1,0:T(8,128)(2,1)S(1)} fusion(bf16[144,16,32]{0,2,1:T(8,128)(2,1)S(1)} %bitcast.63, f32[16,144]{1,0:T(8,128)S(1)} %fusion.29, f32[16,144,144]{1,2,0:T(8,128)} %copy-done.1), kind=kOutput, calls=%fused_computation.13 | convolution fusion | flops 22305168 | bytes 1631232 | tf_op jit(solution)/shard_map/whqk,wkhd->wqhd/dot_general | solution.py:69
  176.9 0.0 copy-done.6
  177.0 0.3 fusion.4
  177.3 3.2 %collective-permute-start.2 = (bf16[1,6,12,512]{3,2,1,0:T(8,128)(2,1)S(1)}, bf16[1,6,12,512]{3,2,1,0:T(8,128)(2,1)S(1)}, u32[]{:S(2)}, u32[]{:S(2)}) collective-permute-start(bf16[1,6,12,512]{3,2,1,0:T(8,128)(2,1)S(1)} %get-tuple-element.17), channel_id=1, source_target_pairs={{480,0},{0,32},{32,64},{64,96},{96,128},{128,160},{160,192},{192,2... | collective-permute-start | bytes 221192 | tf_op jit(solution)/shard_map/ppermute | solution.py:15
  180.5 1.6 collective-permute-done.2
  182.1 1.9 collective-permute-start.3
  184.1 21.3 %collective-permute-done.3 = bf16[1,12,6,512]{3,2,1,0:T(8,128)(2,1)S(1)} collective-permute-done((bf16[1,12,6,512]{3,2,1,0:T(8,128)(2,1)S(1)}, bf16[1,12,6,512]{3,2,1,0:T(8,128)(2,1)S(1)}, u32[]{:S(2)}, u32[]{:S(2)}) %collective-permute-start.3) | collective-permute-done | bytes 73760 | tf_op jit(solution)/shard_map/ppermute | solution.py:15
  205.4 0.8 fusion.7
  (23 shorter events, 0.3 us)
Async XLA Ops:
  0.0 3.4 %copy-start = (bf16[512,1536]{1,0:T(8,128)(2,1)S(1)}, bf16[512,1536]{1,0:T(8,128)(2,1)}, u32[]{:S(2)}) copy-start(bf16[512,1536]{1,0:T(8,128)(2,1)} %param.13) | copy-start | bytes 4718596
  3.4 3.1 %copy-start.9 = (f32[1,16,529]{2,1,0:T(8,128)S(1)}, f32[1,16,529]{2,1,0:T(8,128)}, u32[]{:S(2)}) copy-start(f32[1,16,529]{2,1,0:T(8,128)} %param.15) | copy-start | bytes 101572
  63.3 1.4 copy-start.2
  64.7 0.9 copy-start.7
  65.7 3.1 %copy-start.5 = (bf16[512,512]{1,0:T(8,128)(2,1)S(1)}, bf16[512,512]{1,0:T(8,128)(2,1)}, u32[]{:S(2)}) copy-start(bf16[512,512]{1,0:T(8,128)(2,1)} %param.14) | copy-start | bytes 1572868
  68.8 38.0 %copy-start.10 = (f32[1,16,529]{2,1,0:T(8,128)S(1)}, f32[1,16,529]{2,1,0:T(8,128)}, u32[]{:S(2)}) copy-start(f32[1,16,529]{2,1,0:T(8,128)} %param.19) | copy-start | bytes 101572
  69.5 33.5 %collective-permute-start = (bf16[1,12,6,512]{3,0,2,1:T(2,128)(2,1)S(1)}, bf16[1,12,6,512]{3,0,2,1:T(2,128)(2,1)S(1)}, u32[]{:S(2)}, u32[]{:S(2)}) collective-permute-start(bf16[1,12,6,512]{3,0,2,1:T(2,128)(2,1)S(1)} %get-tuple-element.16), channel_id=1, source_target_pairs={{1,0},{2,1},{3,2},{4,3},{5,4},{6,5},{7,6},{8,7},{9,8},{10,9},{11,1... | collective-permute-start | bytes 221192 | tf_op jit(solution)/shard_map/ppermute | solution.py:15
  104.1 53.7 %collective-permute-start.1 = (bf16[1,6,12,512]{3,0,2,1:T(2,128)(2,1)}, bf16[1,6,12,512]{3,0,2,1:T(2,128)(2,1)}, u32[]{:S(2)}, u32[]{:S(2)}) collective-permute-start(bf16[1,6,12,512]{3,0,2,1:T(2,128)(2,1)} %get-tuple-element.14), channel_id=1, source_target_pairs={{32,0},{64,32},{96,64},{128,96},{160,128},{192,160},{224,192},{256... | collective-permute-start | bytes 221192 | tf_op jit(solution)/shard_map/ppermute | solution.py:15
  145.6 12.2 %copy-start.4 = (bf16[1,6,12,512]{3,0,2,1:T(2,128)(2,1)S(1)}, bf16[1,6,12,512]{3,0,2,1:T(2,128)(2,1)}, u32[]{:S(2)}) copy-start(bf16[1,6,12,512]{3,0,2,1:T(2,128)(2,1)} %get-tuple-element.13) | copy-start | bytes 221188
  145.6 19.9 %copy-start.11 = (f32[512]{0:T(512)S(1)}, f32[512]{0:T(512)}, u32[]{:S(2)}) copy-start(f32[512]{0:T(512)} %param.16) | copy-start | bytes 6148
  157.8 7.6 %copy-start.3 = (bf16[512,1536]{1,0:T(8,128)(2,1)S(1)}, bf16[512,1536]{1,0:T(8,128)(2,1)}, u32[]{:S(2)}) copy-start(bf16[512,1536]{1,0:T(8,128)(2,1)} %param.17) | copy-start | bytes 4718596
  171.5 1.4 copy-start.1
  172.9 0.9 copy-start.8
  173.8 3.1 %copy-start.6 = (bf16[512,512]{1,0:T(8,128)(2,1)S(1)}, bf16[512,512]{1,0:T(8,128)(2,1)}, u32[]{:S(2)}) copy-start(bf16[512,512]{1,0:T(8,128)(2,1)} %param.18) | copy-start | bytes 1572868
  177.3 4.8 %collective-permute-start.2 = (bf16[1,6,12,512]{3,2,1,0:T(8,128)(2,1)S(1)}, bf16[1,6,12,512]{3,2,1,0:T(8,128)(2,1)S(1)}, u32[]{:S(2)}, u32[]{:S(2)}) collective-permute-start(bf16[1,6,12,512]{3,2,1,0:T(8,128)(2,1)S(1)} %get-tuple-element.17), channel_id=1, source_target_pairs={{480,0},{0,32},{32,64},{64,96},{96,128},{128,160},{160,192},{192,2... | collective-permute-start | bytes 221192 | tf_op jit(solution)/shard_map/ppermute | solution.py:15
  182.1 23.2 %collective-permute-start.3 = (bf16[1,12,6,512]{3,2,1,0:T(8,128)(2,1)S(1)}, bf16[1,12,6,512]{3,2,1,0:T(8,128)(2,1)S(1)}, u32[]{:S(2)}, u32[]{:S(2)}) collective-permute-start(bf16[1,12,6,512]{3,2,1,0:T(8,128)(2,1)S(1)} %fusion.15), channel_id=1, source_target_pairs={{31,0},{0,1},{1,2},{2,3},{3,4},{4,5},{5,6},{6,7},{7,8},{8,9},{9,10... | collective-permute-start | bytes 221192 | tf_op jit(solution)/shard_map/ppermute | solution.py:15
where the time goes:
time: 208 us; the launch traced here: 206 us
  local copies, waits for them, and re-layouts  114 us (55%)
  waiting for transfers between devices  35.5 us (17%)
  starting transfers between devices  28.6 us (14%)
  matrix products  16.7 us (8%)
  other arithmetic  11.1 us (5%)
    gather x2, local copies, waits for them, and re-layouts, shards(): bias_two = jnp.take(bias_second[0], rel, axis=1)  50.9 us
    gather x2, local copies, waits for them, and re-layouts, shards(): bias_one = jnp.take(bias_first[0], rel, axis=1)  50.9 us
    ppermute x4, waiting for transfers between devices, shifted(): return lax.ppermute(block, axis, route)  35.5 us
    ppermute x4, starting transfers between devices, shifted(): return lax.ppermute(block, axis, route)  28.6 us
    dot_general x2, matrix products, attend_split(): jnp.einsum('wqhd,wkhd->whqk', query, keys, precision=lax.Precision.HIGHEST)  8.36 us
    dot_general x2, matrix products, attend_split(): jnp.einsum('whqk,wkhd->wqhd', weights, values, preferred_element_type=jnp...  6.21 us
    reduce_sum x2, other arithmetic, norm_rows(): mean = jnp.mean(data, axis=-1, keepdims=True)  4.62 us
  transfers between devices with their start and end apart: 4, of which 3 were waited for; matrix products, arithmetic and copies ran while one was open for 25% of the time, Pallas kernels for 0%

commit v1 on v0

v1 whole, which is shorter than its diff:
```python
import functools
import math

import jax
import jax.numpy as jnp
import numpy as np
from jax import lax
from jax.experimental import pallas as pl
from jax.experimental.pallas import tpu as pltpu
from jax.sharding import PartitionSpec as P

HEADS = 16
WIN = 12
HALF = 6
TOK = 144
DIM = 512
LOG2E = math.log2(math.e)
MESH = pl.DeviceIdType.MESH
F32 = jnp.float32
BF16 = jnp.bfloat16


def own_at(r, c):
    return (c // HALF) * 72 + (r // HALF) * 36 + (r % HALF) * HALF + c % HALF


def constants():
    out = {}
    p0 = np.zeros((288, 192), np.float32)
    back = np.zeros((192, TOK), np.float32)
    for r in range(WIN):
        for c in range(WIN):
            p0[own_at(r, c), r * 16 + c] = 1
            p0[TOK + 143 - (r * WIN + c), r * 16 + c] = 1
            back[r * 16 + c, own_at(r, c)] = 1
    rep = np.zeros((576, TOK), np.float32)
    fold = np.zeros((TOK, 576), np.float32)
    for r in range(WIN):
        for h in range(4):
            for c in range(WIN):
                row = r * 48 + h * WIN + c
                rep[row, 143 - (r * WIN + c)] = 1
                fold[own_at(r, c), row] = 1
    rep2 = np.zeros((2, 288, TOK), np.float32)
    fold2 = np.zeros((2, 192, 288), np.float32)
    strip = np.zeros((2, 288, 416), np.float32)
    for b in range(2):
        for a in range(2):
            for r in range(HALF):
                for h in range(4):
                    for c in range(HALF):
                        row = a * TOK + r * 24 + h * HALF + c
                        rep2[b, row, b * 72 + a * 36 + r * HALF + c] = 1
                        fold2[b, (a * HALF + r) * 16 + b * HALF + c, row] = 1
            for r in range(WIN):
                for c in range(WIN):
                    at = (r % HALF) * HALF + c % HALF
                    own_row = (r >= HALF) == (a == 0)
                    own_col = (c >= HALF) == (b == 0)
                    if own_row and own_col:
                        src = b * 72 + a * 36 + at
                    elif own_col:
                        src = 144 + 48 * a + 8 * b + (4 if a == 0 else 0) + at
                    elif own_row:
                        src = 240 + 8 * (1 - b) + a * 36 + at
                    else:
                        src = 320 + 48 * a + 8 * (1 - b) + (4 if a == 0 else 0) + at
                    strip[b, a * TOK + 143 - (r * WIN + c), src] = 1
    pick = np.zeros((640, 384), np.float32)
    for u in range(23):
        for v in range(WIN):
            pick[u * 23 + v, u * WIN + v] = 1
    order1 = np.zeros((192, 192), np.float32)
    order2 = np.zeros((192, 192), np.float32)
    for h in range(HEADS):
        for c in range(WIN):
            order1[h * WIN + c, c * HEADS + h] = 1
            b = 1 if c < HALF else 0
            order2[b * 96 + h * HALF + c % HALF, c * HEADS + h] = 1
    out["p0"] = p0
    out["pick"] = pick
    out["order1"] = np.concatenate([order1, order1], axis=1)
    out["rep"] = rep
    out["fold"] = fold
    out["back"] = back
    out["order2"] = np.concatenate([order2, order2], axis=1)
    out["rep2"] = rep2
    out["fold2"] = fold2
    out["strip"] = strip
    return out


CONSTS = constants()
CNAMES = list(CONSTS)


def dot(a, b):
    return jnp.dot(a, b, preferred_element_type=F32)


def dot_nt(a, b):
    return lax.dot_general(a, b, (((1,), (1,)), ((), ())), preferred_element_type=F32)


def norm(data, gain):
    mean = jnp.mean(data, axis=-1, keepdims=True)
    centred = data - mean
    var = jnp.mean(centred * centred, axis=-1, keepdims=True)
    return (centred * lax.rsqrt(var + 1e-05) * gain).astype(BF16)


def split(values):
    high = values.astype(BF16)
    return high, (values - high.astype(F32)).astype(BF16)


def head_mask(size, width):
    row = lax.broadcasted_iota(jnp.int32, (4 * size, width), 0)
    lane = lax.broadcasted_iota(jnp.int32, (4 * size, width), 1)
    head = (row >= size).astype(jnp.int32) + (row >= 2 * size).astype(jnp.int32) + (row >= 3 * size).astype(jnp.int32)
    return head == ((lane // 32) & 3)


def masked(values, size):
    rows, width = values.shape
    mask = head_mask(size, width)
    kept = jnp.where(mask[None], values.reshape(rows // (4 * size), 4 * size, width), 0.0)
    return kept.reshape(rows, width).astype(BF16)


def offsets_table(table, padded, pick, order):
    padded[...] = jnp.zeros_like(padded)
    padded[:, :529] = table
    flat = padded[...] * LOG2E
    rows = jnp.concatenate([flat] + [pltpu.roll(flat, 640 - c, 1) for c in range(1, WIN)], axis=0)
    high, low = split(rows)
    parts = jnp.concatenate([dot(high, pick).astype(BF16), dot(low, pick).astype(BF16)], axis=0)
    return dot(order, parts)


def attend(qhi, qlo, khi, klo, val, bias, size):
    parts = []
    ones = jnp.ones((val.shape[0], 128), BF16)
    for g in range(4):
        at = slice(128 * g, 128 * g + 128)
        left = jnp.concatenate([qhi[:, at], qlo[:, at], qhi[:, at]], axis=1)
        right = jnp.concatenate([khi[:, at], khi[:, at], klo[:, at]], axis=1)
        scores = dot_nt(left, right) + bias(g)
        top = jnp.max(scores, axis=-1, keepdims=True)
        expo = jnp.exp2(scores - top).astype(BF16)
        both = dot(expo, jnp.concatenate([val[:, at], ones], axis=1))
        parts.append(masked(both[:, :128] / both[:, 128:], size))
    return jnp.concatenate(parts, axis=1)


def kernel(
    nlat, nlon, tok_h, gain1_h, wqkv1_h, wproj1_h, bias1_h, gain2_h, wqkv2_h, wproj2_h, bias2_h, *rest
):
    nc = len(CNAMES)
    const_h = dict(zip(CNAMES, rest[:nc]))
    out_h = rest[nc]
    (tok, gain1, wqkv1, wproj1, tab1, gain2, wqkv2, wproj2, tab2, tabn), rest = rest[nc + 1 : nc + 11], rest[nc + 11 :]
    const = dict(zip(CNAMES, rest[:nc]))
    (
        xpad, tpad, bias1, bias2, near, halo_lon, halo_lat, corner, result,
        in_sem, out_sem, lon_send, lon_recv, lat_send, lat_recv, cor_send, cor_recv, tab_send, tab_recv,
    ) = rest[nc:]

    lat = lax.axis_index("lat")
    lon = lax.axis_index("lon")
    north = lax.rem(lat + nlat - 1, nlat)
    south = lax.rem(lat + 1, nlat)
    west = lax.rem(lon + nlon - 1, nlon)
    east = lax.rem(lon + 1, nlon)
    has_n = lat > 0
    has_s = lat < nlat - 1

    barrier = pltpu.get_barrier_semaphore()
    for peer in ((lat, west), (lat, east), (north, lon), (south, lon)):
        pl.semaphore_signal(barrier, inc=1, device_id=peer, device_id_type=MESH)

    loads = {}
    order = [
        ("tok", tok_h, tok), ("p0", const_h["p0"], const["p0"]), ("tab1", bias1_h, tab1),
        ("pick", const_h["pick"], const["pick"]), ("gain1", gain1_h, gain1), ("order1", const_h["order1"], const["order1"]),
        ("wqkv1", wqkv1_h, wqkv1), ("rep", const_h["rep"], const["rep"]), ("fold", const_h["fold"], const["fold"]),
        ("wproj1", wproj1_h, wproj1), ("gain2", gain2_h, gain2), ("tab2", bias2_h, tab2),
        ("order2", const_h["order2"], const["order2"]), ("wqkv2", wqkv2_h, wqkv2), ("rep2", const_h["rep2"], const["rep2"]),
        ("strip", const_h["strip"], const["strip"]), ("back", const_h["back"], const["back"]),
        ("fold2", const_h["fold2"], const["fold2"]), ("wproj2", wproj2_h, wproj2),
    ]
    for i, (name, src, dst) in enumerate(order):
        loads[name] = pltpu.make_async_copy(src, dst, in_sem.at[i])
        loads[name].start()

    def get(name):
        loads[name].wait()

    get("tab1")
    get("pick")
    get("order1")
    table = offsets_table(tab1[0], tpad, const["pick"][...], const["order1"][...])
    for r in range(WIN):
        moved = table[:, WIN * r : WIN * r + TOK]
        for g in range(4):
            bias1[g, 48 * r : 48 * r + 48, :] = moved[48 * g : 48 * g + 48]

    get("tok")
    get("p0")
    xpad[...] = jnp.zeros_like(xpad)
    for r in range(WIN):
        xpad[16 * r : 16 * r + WIN, :] = tok[0, r]
    both = dot(const["p0"][...], xpad[...])
    mine = both[:TOK]
    get("gain1")
    normed = norm(both[TOK:], gain1[...])
    get("wqkv1")
    scale = LOG2E / math.sqrt(32.0)
    flat = dot(normed, wqkv1[...])
    qhi, qlo = split(flat[:, :DIM] * scale)
    khi, klo = split(flat[:, DIM : 2 * DIM])
    val = flat[:, 2 * DIM :].astype(BF16)
    get("rep")
    rep = const["rep"][...]
    heads = attend(
        masked(dot(rep, qhi), WIN), masked(dot(rep, qlo), WIN), khi, klo, val, lambda g: bias1[g], WIN
    )
    get("fold")
    get("wproj1")
    heads = dot(const["fold"][...], heads).astype(BF16)
    first = (mine + dot(heads, wproj1[...])).astype(BF16)
    get("gain2")
    normed = norm(first.astype(F32), gain2[...])
    own = result
    own[...] = normed

    get("tab2")
    pl.semaphore_wait(barrier, 4)

    def remote(src, dst, send, recv, peer):
        return pltpu.make_async_remote_copy(
            src_ref=src, dst_ref=dst, send_sem=send, recv_sem=recv, device_id=peer, device_id_type=MESH
        )

    to_w = remote(own.at[pl.ds(0, 80)], halo_lon.at[1], lon_send.at[0], lon_recv.at[1], (lat, west))
    to_e = remote(own.at[pl.ds(64, 80)], halo_lon.at[0], lon_send.at[1], lon_recv.at[0], (lat, east))
    to_w.start()
    to_e.start()
    to_n = [
        remote(own.at[pl.ds(64 * b, 48)], halo_lat.at[1, b], lat_send.at[0, b], lat_recv.at[1, b], (north, lon))
        for b in range(2)
    ]
    to_s = [
        remote(own.at[pl.ds(32 + 64 * b, 48)], halo_lat.at[0, b], lat_send.at[1, b], lat_recv.at[0, b], (south, lon))
        for b in range(2)
    ]

    @pl.when(has_n)
    def _():
        for copy in to_n:
            copy.start()

    @pl.when(has_s)
    def _():
        for copy in to_s:
            copy.start()

    send_tab = remote(tab2, tabn, tab_send, tab_recv, (south, lon))
    send_tab.start()

    @pl.when(lat == 0)
    def _():
        halo_lat[0] = jnp.zeros((2, 48, DIM), BF16)
        corner[0] = jnp.zeros((2, 48, DIM), BF16)

    @pl.when(lat == nlat - 1)
    def _():
        halo_lat[1] = jnp.zeros((2, 48, DIM), BF16)
        corner[1] = jnp.zeros((2, 48, DIM), BF16)

    get("order2")

    def window_bias(a, ref):
        table = offsets_table(ref[0], tpad, const["pick"][...], const["order2"][...])
        cut = jnp.logical_not(has_n if a == 0 else has_s)
        lane = lax.broadcasted_iota(jnp.int32, (1, TOK), 1)
        other = (lane >= 72) if a == 0 else (lane < 72)
        shut = jnp.where(other, jnp.where(cut, -1e30, 0.0), 0.0)
        for r in range(HALF):
            at = WIN * (r + (HALF if a == 0 else 0))
            moved = table[:, at : at + TOK] + shut
            for b in range(2):
                for g in range(4):
                    bias2[a, b, g, 24 * r : 24 * r + 24, :] = moved[96 * b + 24 * g : 96 * b + 24 * g + 24]

    window_bias(1, tab2)
    get("wqkv2")
    qhi, qlo = split(dot(normed, wqkv2[:, :DIM]) * scale)
    get("back")
    residual = dot(const["back"][...], first)
    get("rep2")
    get("strip")
    get("fold2")

    far_w = lax.rem(lon, nlon // 2) == 0
    side_far = jnp.where(far_w, 0, 1)
    side_near = 1 - side_far

    def relay(b):
        remote(own.at[pl.ds(0, 80)], halo_lon.at[b], lon_send.at[0], lon_recv.at[b], (lat, west)).wait_recv()

        @pl.when(has_n)
        def _():
            remote(halo_lon.at[b, pl.ds(0, 48)], corner.at[1, b], cor_send.at[0, b], cor_recv.at[1, b], (north, lon)).start()

        @pl.when(has_s)
        def _():
            remote(halo_lon.at[b, pl.ds(32, 48)], corner.at[0, b], cor_send.at[1, b], cor_recv.at[0, b], (south, lon)).start()

    def settle(b):
        for a, has in ((0, has_n), (1, has_s)):
            @pl.when(has)
            def _(a=a):
                remote(own.at[pl.ds(0, 48)], corner.at[a, b], cor_send.at[0, b], cor_recv.at[a, b], (north, lon)).wait_recv()

    def side(b):
        gathered = jnp.concatenate(
            [own[...], halo_lat[0, b], halo_lat[1, b], halo_lon[b], corner[0, b], corner[1, b]], axis=0
        )
        keys = dot(const["strip"][b], gathered).astype(BF16)
        flat = dot(keys, wqkv2[:, DIM:])
        khi, klo = split(flat[:, :DIM])
        val = flat[:, DIM:].astype(BF16)
        rep = const["rep2"][b]
        ahi = masked(dot(rep, qhi), HALF)
        alo = masked(dot(rep, qlo), HALF)
        parts = []
        for a in range(2):
            at = slice(TOK * a, TOK * a + TOK)
            parts.append(
                attend(ahi[at], alo[at], khi[at], klo[at], val[at], lambda g, a=a: bias2[a, b, g], HALF)
            )
        return dot(const["fold2"][b], jnp.concatenate(parts, axis=0))

    relay(side_near)
    remote(tab2, tabn, tab_send, tab_recv, (south, lon)).wait_recv()
    window_bias(0, tabn)
    for a, has in ((0, has_n), (1, has_s)):
        @pl.when(has)
        def _(a=a):
            for b in range(2):
                remote(own.at[pl.ds(0, 48)], halo_lat.at[a, b], lat_send.at[0, b], lat_recv.at[a, b], (north, lon)).wait_recv()

    settle(side_near)
    near[...] = side(side_near)
    relay(side_far)
    settle(side_far)
    heads = (near[...] + side(side_far)).astype(BF16)
    get("wproj2")
    mixed = (residual + dot(heads, wproj2[...])).astype(BF16)
    for r in range(WIN):
        tok[0, r] = mixed[16 * r : 16 * r + WIN]
    store = pltpu.make_async_copy(tok, out_h, out_sem)
    store.start()

    to_w.wait_send()
    to_e.wait_send()
    send_tab.wait_send()

    @pl.when(has_n)
    def _():
        for b in range(2):
            to_n[b].wait_send()
            remote(own.at[pl.ds(0, 48)], corner.at[1, b], cor_send.at[0, b], cor_recv.at[1, b], (north, lon)).wait_send()

    @pl.when(has_s)
    def _():
        for b in range(2):
            to_s[b].wait_send()
            remote(own.at[pl.ds(0, 48)], corner.at[0, b], cor_send.at[1, b], cor_recv.at[0, b], (south, lon)).wait_send()

    store.wait()


def shards(tokens, gain1, wqkv1, wproj1, bias1, gain2, wqkv2, wproj2, bias2):
    nlat = lax.axis_size("lat")
    nlon = lax.axis_size("lon")
    consts = [jnp.asarray(CONSTS[name], BF16) for name in CNAMES]
    dma = pltpu.SemaphoreType.DMA
    vmem = pltpu.VMEM
    args = [tokens, gain1.reshape(1, DIM), wqkv1, wproj1, bias1, gain2.reshape(1, DIM), wqkv2, wproj2, bias2]
    scratch = [vmem(x.shape, x.dtype) for x in args] + [vmem(bias2.shape, F32)]
    scratch += [vmem(x.shape, BF16) for x in consts]
    scratch += [
        vmem((192, DIM), BF16),
        vmem((HEADS, 640), F32),
        vmem((4, 576, TOK), F32),
        vmem((2, 2, 4, TOK, TOK), F32),
        vmem((192, DIM), F32),
        vmem((2, 80, DIM), BF16),
        vmem((2, 2, 48, DIM), BF16),
        vmem((2, 2, 48, DIM), BF16),
        vmem((TOK, DIM), BF16),
        dma((len(args) + len(consts),)),
        dma(()),
        dma((2,)), dma((2,)),
        dma((2, 2)), dma((2, 2)),
        dma((2, 2)), dma((2, 2)),
        dma(()), dma(()),
    ]
    anywhere = pl.BlockSpec(memory_space=pltpu.HBM)
    return pl.pallas_call(
        functools.partial(kernel, nlat, nlon),
        out_shape=jax.ShapeDtypeStruct(tokens.shape, BF16),
        in_specs=[anywhere] * (len(args) + len(consts)),
        out_specs=anywhere,
        scratch_shapes=scratch,
        compiler_params=pltpu.CompilerParams(
            collective_id=0, has_side_effects=True, vmem_limit_bytes=62 * 1024 * 1024
        ),
        cost_estimate=pl.CostEstimate(flops=2_000_000_000, bytes_accessed=8_000_000, transcendentals=700_000),
        name="pair",
    )(*args, *consts)


def solution(mesh):
    placed = (
        P(None, "lat", "lon", None), P(), P(), P(), P("lat", None, None), P(), P(), P(), P("lat", None, None),
    )
    return jax.shard_map(
        shards, mesh=mesh, in_specs=placed, out_specs=P(None, "lat", "lon", None), check_vma=False
    )
```

time: 208 us -> 43.2 us (0.21)
  local copies, waits for them, and re-layouts: 114 us -> 1.62 us
  Pallas kernels: 0 us -> 41.4 us
  waiting for transfers between devices: 35.5 us -> 0 us
  starting transfers between devices: 28.6 us -> 0 us
  matrix products: 16.7 us -> 0 us
  other arithmetic: 11.1 us -> 0 us
    gather x4 -> x0, local copies, waits for them, and re-layouts: 102 us -> none  [the longest x2 50.9 us: shards(): bias_two = jnp.take(bias_second[0], rel, axis=1)]
    pallas_call x0 -> x1, Pallas kernels: none -> 41.4 us  [shards(): pl.pallas_call(functools.partial(kernel, nlat, nlon), out_shape=jax.Shape...]
    ppermute x4 -> x0, waiting for transfers between devices: 35.5 us -> none  [shifted(): return lax.ppermute(block, axis, route)]
    ppermute x4 -> x0, starting transfers between devices: 28.6 us -> none  [shifted(): return lax.ppermute(block, axis, route)]
    dot_general x8 -> x0, matrix products: 16.7 us -> none  [the longest x2 8.36 us: attend_split(): jnp.einsum('wqhd,wkhd->whqk', query, keys, precision=lax.Precision.HIGHEST)]
    reduce_sum x4 -> x0, other arithmetic: 7.73 us -> none  [the longest x2 4.62 us: norm_rows(): mean = jnp.mean(data, axis=-1, keepdims=True)]
    slice x12 -> x0, local copies, waits for them, and re-layouts: 4.61 us -> none  [the longest x4 2.16 us: attend_tokens(): keys = mixed[..., width:2 * width]]
    convert_element_type x3 -> x0, local copies, waits for them, and re-layouts: 3.07 us -> none  [the longest x2 2.04 us: shards(): wins.astype(jnp.float32)]
  transfers between devices with their start and end apart: 4 -> 0, of which waited for: 3 -> 0; matrix products, arithmetic and copies ran while one was open for 25% -> 0% of each run, Pallas kernels for 0% -> 0%
where the time goes in v1:
time: 43.2 us; the launch traced here: 43 us
  Pallas kernels  41.4 us (96%)
  local copies, waits for them, and re-layouts  1.62 us (4%)
    pallas_call x1, Pallas kernels, shards(): pl.pallas_call(functools.partial(kernel, nlat, nlon), out_shape=jax.Shape...  41.4 us
    unnamed x1, local copies, waits for them, and re-layouts  1.62 us

profile of v1, /device:TPU:1, one launch (start us, length us, event | category | flops | bytes accessed | tf_op | source)
XLA Modules:
  0.0 43.0 jit_solution(12672087327141284387)
XLA Ops:
  0.0 41.4 %pair.1 = bf16[1,12,12,512]{3,2,1,0:T(8,128)(2,1)} custom-call(bf16[1,12,12,512]{3,2,1,0:T(8,128)(2,1)} %tok_h.1, f32[1,512]{1,0:T(1,128)} %bitcast.2, bf16[512,1536]{1,0:T(8,128)(2,1)} %wqkv1_h.1, bf16[512,512]{1,0:T(8,128)(2,1)} %wproj1_h.1, f32[1,16,529]{2,1,0:T(8,128)} %bias1_h.1, f32[1,512]{1,0:T(1,128)} %bitcast.3, bf16[512,1536]{1,0:T(8,128)(2,1)} %wqkv2_h.1, ...), custom_call_target="tpu_custom_call" | custom-call | flops 2000000000 | bytes 8000000 | tf_op jit(solution)/shard_map/pair/pallas_call | solution.py:412
  41.4 1.6 %copy.21 = bf16[1,12,12,512]{3,2,1,0:T(8,128)(2,1)} copy(bf16[1,12,12,512]{3,2,1,0:T(8,128)(2,1)} %pair.1) | data formatting | bytes 294912

commit v2 on v1

v2 whole, which is shorter than its diff:
```python
import functools
import math

import jax
import jax.numpy as jnp
import numpy as np
from jax import lax
from jax.experimental import pallas as pl
from jax.experimental.pallas import tpu as pltpu
from jax.sharding import PartitionSpec as P

HEADS = 16
WIN = 12
HALF = 6
TOK = 144
DIM = 512
LOG2E = math.log2(math.e)
MESH = pl.DeviceIdType.MESH
F32 = jnp.float32
BF16 = jnp.bfloat16


def own_at(r, c):
    return (c // HALF) * 72 + (r // HALF) * 36 + (r % HALF) * HALF + c % HALF


def constants():
    p0 = np.zeros((288, 192), np.float32)
    back = np.zeros((192, TOK), np.float32)
    rep = np.zeros((576, TOK), np.float32)
    fold = np.zeros((TOK, 576), np.float32)
    for r in range(WIN):
        for c in range(WIN):
            flipped = 143 - (c * WIN + r)
            p0[own_at(r, c), r * 16 + c] = 1
            p0[TOK + flipped, r * 16 + c] = 1
            back[r * 16 + c, own_at(r, c)] = 1
            for h in range(4):
                rep[c * 48 + h * WIN + r, flipped] = 1
                fold[own_at(r, c), c * 48 + h * WIN + r] = 1
    rep2 = np.zeros((576, TOK), np.float32)
    fold2 = np.zeros((2, 192, 288), np.float32)
    early = np.zeros((288, 304), np.float32)
    late = np.zeros((TOK, 160), np.float32)
    for b in range(2):
        for a in range(2):
            for c in range(HALF):
                for r in range(HALF):
                    at = r * HALF + c
                    for h in range(4):
                        row = a * TOK + c * 24 + h * HALF + r
                        rep2[b * 288 + row, b * 72 + a * 36 + at] = 1
                        fold2[b, (a * HALF + r) * 16 + b * HALF + c, row] = 1
                    for whole in (r, r + HALF):
                        key = (HALF - 1 - c) * WIN + WIN - 1 - whole
                        mine = (whole >= HALF) == (a == 0)
                        src = b * 72 + a * 36 + at if mine else 144 + 40 * (2 * a + b) + at
                        early[b * 144 + a * 72 + key, src] = 1
                        late[a * 72 + key, 40 * a + at if mine else 80 + 40 * a + at] = 1
    pick = np.zeros((384, 384), np.float32)
    for v in range(23):
        for r in range(WIN):
            pick[r * 23 + v, v * WIN + r] = 1
    order1 = np.zeros((192, 192), np.float32)
    order2 = np.zeros((96, 96), np.float32)
    for h in range(HEADS):
        for r in range(WIN):
            order1[h * WIN + r, r * HEADS + h] = 1
        for r in range(HALF):
            order2[h * HALF + r, r * HEADS + h] = 1
    return {
        "p0": p0,
        "pick": pick,
        "order1": np.concatenate([order1, order1], axis=1),
        "rep": rep,
        "fold": fold,
        "back": back,
        "order2": np.concatenate([order2, order2], axis=1),
        "rep2": rep2,
        "early": early,
        "late": late,
        "fold2": fold2,
    }


CONSTS = constants()
CNAMES = list(CONSTS)


def dot(a, b):
    return jnp.dot(a, b, preferred_element_type=F32)


def dot_nt(a, b):
    return lax.dot_general(a, b, (((1,), (1,)), ((), ())), preferred_element_type=F32)


def norm(data, gain):
    mean = jnp.mean(data, axis=-1, keepdims=True)
    centred = data - mean
    var = jnp.mean(centred * centred, axis=-1, keepdims=True)
    return (centred * lax.rsqrt(var + 1e-05) * gain).astype(BF16)


def split(values):
    high = values.astype(BF16)
    return high, (values - high.astype(F32)).astype(BF16)


def head_mask(size, width):
    row = lax.broadcasted_iota(jnp.int32, (4 * size, width), 0)
    lane = lax.broadcasted_iota(jnp.int32, (4 * size, width), 1)
    head = (row >= size).astype(jnp.int32) + (row >= 2 * size).astype(jnp.int32) + (row >= 3 * size).astype(jnp.int32)
    return head == ((lane // 32) & 3)


def masked(values, size):
    rows, width = values.shape
    mask = head_mask(size, width)
    kept = jnp.where(mask[None], values.reshape(rows // (4 * size), 4 * size, width), 0.0)
    return kept.reshape(rows, width).astype(BF16)


def offsets_table(table, padded, pick, order, start, count):
    padded[...] = jnp.zeros_like(padded)
    padded[:, :529] = table
    flat = padded[...] * LOG2E
    moved = [pltpu.roll(flat, (640 - 23 * r) % 640, 1) if r else flat for r in range(start, start + count)]
    rows = jnp.concatenate([m[:, :384] for m in moved], axis=0)
    high, low = split(rows)
    parts = jnp.concatenate([dot(high, pick).astype(BF16), dot(low, pick).astype(BF16)], axis=0)
    return dot(order, parts)


def attend(qhi, qlo, khi, klo, val, bias, size):
    parts = []
    ones = jnp.ones((val.shape[0], 128), BF16)
    for g in range(4):
        at = slice(128 * g, 128 * g + 128)
        left = jnp.concatenate([qhi[:, at], qlo[:, at], qhi[:, at]], axis=1)
        right = jnp.concatenate([khi[:, at], khi[:, at], klo[:, at]], axis=1)
        scores = dot_nt(left, right) + bias(g)
        top = jnp.max(scores, axis=-1, keepdims=True)
        expo = jnp.exp2(scores - top).astype(BF16)
        both = dot(expo, jnp.concatenate([val[:, at], ones], axis=1))
        parts.append(masked(both[:, :128] / both[:, 128:], size))
    return jnp.concatenate(parts, axis=1)


def kernel(
    nlat, nlon, tok_h, gain1_h, wqkv1_h, wproj1_h, bias1_h, gain2_h, wqkv2_h, wproj2_h, bias2_h, *rest
):
    nc = len(CNAMES)
    const_h = dict(zip(CNAMES, rest[:nc]))
    out_h = rest[nc]
    (tok, gain1, wqkv1, wproj1, tab1, gain2, wqkv2, wproj2, tab2, tabn), rest = rest[nc + 1 : nc + 11], rest[nc + 11 :]
    const = dict(zip(CNAMES, rest[:nc]))
    (
        xpad, tpad, bias1, bias2, near, halo_lon, halo_lat, corner, own, pack, packed, unpack, keyval, ahi, alo,
        in_sem, out_sem, lon_send, lon_recv, lat_send, lat_recv, cor_send, cor_recv, tab_send, tab_recv,
    ) = rest[nc:]

    lat = lax.axis_index("lat")
    lon = lax.axis_index("lon")
    north = lax.rem(lat + nlat - 1, nlat)
    south = lax.rem(lat + 1, nlat)
    west = lax.rem(lon + nlon - 1, nlon)
    east = lax.rem(lon + 1, nlon)
    has_n = lat > 0
    has_s = lat < nlat - 1

    barrier = pltpu.get_barrier_semaphore()
    for peer in ((lat, west), (lat, east), (north, lon), (south, lon)):
        pl.semaphore_signal(barrier, inc=1, device_id=peer, device_id_type=MESH)

    loads = {}
    early_loads = [
        ("tab1", bias1_h, tab1), ("pick", const_h["pick"], const["pick"]), ("order1", const_h["order1"], const["order1"]),
        ("tok", tok_h, tok), ("p0", const_h["p0"], const["p0"]), ("gain1", gain1_h, gain1),
        ("wqkv1", wqkv1_h, wqkv1), ("rep", const_h["rep"], const["rep"]), ("fold", const_h["fold"], const["fold"]),
        ("wproj1", wproj1_h, wproj1), ("gain2", gain2_h, gain2), ("tab2", bias2_h, tab2),
    ]
    late_loads = [
        ("order2", const_h["order2"], const["order2"]), ("wqkv2", wqkv2_h, wqkv2), ("rep2", const_h["rep2"], const["rep2"]),
        ("back", const_h["back"], const["back"]), ("early", const_h["early"], const["early"]),
        ("late", const_h["late"], const["late"]), ("fold2", const_h["fold2"], const["fold2"]), ("wproj2", wproj2_h, wproj2),
    ]
    for i, (name, src, dst) in enumerate(early_loads + late_loads):
        loads[name] = pltpu.make_async_copy(src, dst, in_sem.at[i])
    for name, _, _ in early_loads:
        loads[name].start()

    def get(name):
        loads[name].wait()

    get("tab1")
    get("pick")
    get("order1")
    table = offsets_table(tab1[0], tpad, const["pick"][...], const["order1"][...], 0, WIN)
    for c in range(WIN):
        moved = table[:, WIN * c : WIN * c + TOK]
        for g in range(4):
            bias1[g, 48 * c : 48 * c + 48, :] = moved[48 * g : 48 * g + 48]

    get("tok")
    get("p0")
    xpad[...] = jnp.zeros_like(xpad)
    for r in range(WIN):
        xpad[16 * r : 16 * r + WIN, :] = tok[0, r]
    both = dot(const["p0"][...], xpad[...])
    mine = both[:TOK]
    get("gain1")
    normed = norm(both[TOK:], gain1[...])
    get("wqkv1")
    scale = LOG2E / math.sqrt(32.0)
    flat = dot(normed, wqkv1[...])
    qhi, qlo = split(flat[:, :DIM] * scale)
    khi, klo = split(flat[:, DIM : 2 * DIM])
    val = flat[:, 2 * DIM :].astype(BF16)
    get("rep")
    for name, _, _ in late_loads:
        loads[name].start()
    rep = const["rep"][...]
    heads = attend(
        masked(dot(rep, qhi), WIN), masked(dot(rep, qlo), WIN), khi, klo, val, lambda g: bias1[g], WIN
    )
    get("fold")
    get("wproj1")
    heads = dot(const["fold"][...], heads).astype(BF16)
    first = (mine + dot(heads, wproj1[...])).astype(BF16)
    get("gain2")
    normed = norm(first.astype(F32), gain2[...])
    own[...] = normed
    wide = normed.astype(F32)
    for a in range(2):
        for b in range(2):
            for j in range(4):
                at = 72 * b + 36 * a
                pack[a, b, 36 * j : 36 * j + 36, :] = wide[at : at + 36, 128 * j : 128 * j + 128]
    packed[...] = pack[...].astype(BF16)

    side_far = jnp.where(lax.rem(lon, nlon // 2) == 0, 0, 1)
    side_near = 1 - side_far
    border = jnp.logical_or(lax.rem(lon, nlon // 2) == 0, lax.rem(lon, nlon // 2) == nlon // 2 - 1)
    part0 = lax.rem(lat, 2)
    get("tab2")
    pl.semaphore_wait(barrier, 4)

    def remote(src, dst, send, recv, peer):
        return pltpu.make_async_remote_copy(
            src_ref=src, dst_ref=dst, send_sem=send, recv_sem=recv, device_id=peer, device_id_type=MESH
        )

    def edge(b, a):
        peer = jnp.where(b == 0, west, east)
        return remote(packed.at[a, b], halo_lon.at[1 - b, a], lon_send.at[b, a], lon_recv.at[1 - b, a], (lat, peer))

    for b in (side_far, side_near):
        for a in (part0, 1 - part0):
            edge(b, a).start()
    to_n = remote(packed.at[0], halo_lat.at[1], lat_send.at[0], lat_recv.at[1], (north, lon))
    to_s = remote(packed.at[1], halo_lat.at[0], lat_send.at[1], lat_recv.at[0], (south, lon))

    @pl.when(has_n)
    def _():
        to_n.start()

    @pl.when(has_s)
    def _():
        to_s.start()

    send_tab = remote(tab2, tabn, tab_send, tab_recv, (south, lon))
    send_tab.start()

    for a, has in ((0, has_n), (1, has_s)):
        @pl.when(jnp.logical_not(has))
        def _(a=a):
            halo_lat[a] = jnp.zeros((2, TOK, 128), BF16)
            for b in range(2):
                corner[b, a] = jnp.zeros((TOK, 128), BF16)

    get("order2")

    def window_bias(a, ref):
        start = HALF if a == 0 else 0
        table = offsets_table(ref[0], tpad, const["pick"][...], const["order2"][...], start, HALF)
        cut = jnp.logical_not(has_n if a == 0 else has_s)
        lane = lax.rem(lax.broadcasted_iota(jnp.int32, (1, TOK), 1), WIN)
        other = (lane >= HALF) if a == 0 else (lane < HALF)
        shut = jnp.where(other, jnp.where(cut, -1e30, 0.0), 0.0)
        for c in range(WIN):
            moved = table[:, WIN * c : WIN * c + TOK] + shut
            b = 0 if c >= HALF else 1
            row = 24 * (c % HALF)
            for g in range(4):
                bias2[a, b, g, row : row + 24, :] = moved[24 * g : 24 * g + 24]

    def relay(b):
        for a in (part0, 1 - part0):
            remote(packed.at[a, b], halo_lon.at[b, a], lon_send.at[b, a], lon_recv.at[b, a], (lat, west)).wait_recv()
            peer = jnp.where(a == 0, north, south)

            @pl.when(jnp.where(a == 0, lat > 0, lat < nlat - 1))
            def _(a=a, peer=peer):
                remote(
                    halo_lon.at[b, a], corner.at[b, 1 - a], cor_send.at[b, a], cor_recv.at[b, 1 - a], (peer, lon)
                ).start()

    def settle(b):
        for a, has in ((0, has_n), (1, has_s)):
            @pl.when(has)
            def _(a=a):
                remote(
                    halo_lon.at[b, a], corner.at[b, a], cor_send.at[b, a], cor_recv.at[b, a], (north, lon)
                ).wait_recv()

    def tokens_of(quadrants):
        for i, ref in enumerate(quadrants):
            data = ref[...].astype(F32)
            for j in range(4):
                unpack[40 * i : 40 * i + 36, 128 * j : 128 * j + 128] = data[36 * j : 36 * j + 36]
        return unpack[...].astype(BF16)

    def side(b):
        new = tokens_of([halo_lon.at[b, 0], halo_lon.at[b, 1], corner.at[b, 0], corner.at[b, 1]])
        new = dot(dot(const["late"][...], new).astype(BF16), wqkv2[:, DIM:])
        for a in range(2):
            keyval[b, a, pl.ds(pl.multiple_of(72 * (1 - b), 8), 72), :] = new[72 * a : 72 * a + 72]
        parts = []
        for a in range(2):
            khi, klo = split(keyval[b, a, :, :DIM])
            val = keyval[b, a, :, DIM:].astype(BF16)
            at = pl.ds(TOK * a, TOK)
            parts.append(
                attend(ahi[b, at], alo[b, at], khi, klo, val, lambda g, a=a: bias2[a, b, g], HALF)
            )
        return dot(const["fold2"][b], jnp.concatenate(parts, axis=0))

    unpack[...] = jnp.zeros_like(unpack)
    window_bias(1, tab2)
    get("wqkv2")
    qhi, qlo = split(dot(normed, wqkv2[:, :DIM]) * scale)
    get("rep2")
    rep = const["rep2"][...]
    ahi[...] = masked(dot(rep, qhi), HALF).reshape(2, 288, DIM)
    alo[...] = masked(dot(rep, qlo), HALF).reshape(2, 288, DIM)
    get("back")
    residual = dot(const["back"][...], first)
    get("early")
    get("late")
    get("fold2")
    get("wproj2")

    relay(side_near)

    @pl.when(jnp.logical_not(border))
    def _():
        relay(side_far)

    remote(tab2, tabn, tab_send, tab_recv, (south, lon)).wait_recv()
    window_bias(0, tabn)
    for a, has in ((0, has_n), (1, has_s)):
        @pl.when(has)
        def _(a=a):
            remote(packed.at[a], halo_lat.at[a], lat_send.at[a], lat_recv.at[a], (north, lon)).wait_recv()

    known = jnp.concatenate(
        [own[...], tokens_of([halo_lat.at[0, 0], halo_lat.at[0, 1], halo_lat.at[1, 0], halo_lat.at[1, 1]])], axis=0
    )
    known = dot(dot(const["early"][...], known).astype(BF16), wqkv2[:, DIM:])
    for b in range(2):
        for a in range(2):
            at = 144 * b + 72 * a
            keyval[b, a, 72 * b : 72 * b + 72, :] = known[at : at + 72]

    settle(side_near)
    near[...] = side(side_near)

    @pl.when(border)
    def _():
        relay(side_far)

    settle(side_far)
    heads = (near[...] + side(side_far)).astype(BF16)
    mixed = (residual + dot(heads, wproj2[...])).astype(BF16)
    for r in range(WIN):
        tok[0, r] = mixed[16 * r : 16 * r + WIN]
    store = pltpu.make_async_copy(tok, out_h, out_sem)
    store.start()

    for b in range(2):
        for a in range(2):
            edge(b, a).wait_send()
    send_tab.wait_send()
    for a, has, copy, peer in ((0, has_n, to_n, north), (1, has_s, to_s, south)):
        @pl.when(has)
        def _(a=a, copy=copy, peer=peer):
            copy.wait_send()
            for b in range(2):
                remote(
                    halo_lon.at[b, a], corner.at[b, 1 - a], cor_send.at[b, a], cor_recv.at[b, 1 - a], (peer, lon)
                ).wait_send()

    store.wait()


def shards(tokens, gain1, wqkv1, wproj1, bias1, gain2, wqkv2, wproj2, bias2):
    nlat = lax.axis_size("lat")
    nlon = lax.axis_size("lon")
    consts = [jnp.asarray(CONSTS[name], BF16) for name in CNAMES]
    dma = pltpu.SemaphoreType.DMA
    vmem = pltpu.VMEM
    args = [tokens, gain1.reshape(1, DIM), wqkv1, wproj1, bias1, gain2.reshape(1, DIM), wqkv2, wproj2, bias2]
    scratch = [vmem(x.shape, x.dtype) for x in args] + [vmem(bias2.shape, F32)]
    scratch += [vmem(x.shape, BF16) for x in consts]
    scratch += [
        vmem((192, DIM), BF16),
        vmem((HEADS, 640), F32),
        vmem((4, 576, TOK), F32),
        vmem((2, 2, 4, TOK, TOK), F32),
        vmem((192, DIM), F32),
        vmem((2, 2, TOK, 128), BF16),
        vmem((2, 2, TOK, 128), BF16),
        vmem((2, 2, TOK, 128), BF16),
        vmem((TOK, DIM), BF16),
        vmem((2, 2, TOK, 128), F32),
        vmem((2, 2, TOK, 128), BF16),
        vmem((160, DIM), F32),
        vmem((2, 2, TOK, 2 * DIM), F32),
        vmem((2, 288, DIM), BF16),
        vmem((2, 288, DIM), BF16),
        dma((len(args) + len(consts),)),
        dma(()),
        dma((2, 2)), dma((2, 2)),
        dma((2,)), dma((2,)),
        dma((2, 2)), dma((2, 2)),
        dma(()), dma(()),
    ]
    anywhere = pl.BlockSpec(memory_space=pl.ANY)
    return pl.pallas_call(
        functools.partial(kernel, nlat, nlon),
        out_shape=jax.ShapeDtypeStruct(tokens.shape, BF16),
        in_specs=[anywhere] * (len(args) + len(consts)),
        out_specs=anywhere,
        scratch_shapes=scratch,
        compiler_params=pltpu.CompilerParams(
            collective_id=0, has_side_effects=True, vmem_limit_bytes=62 * 1024 * 1024
        ),
        cost_estimate=pl.CostEstimate(flops=2_000_000_000, bytes_accessed=8_000_000, transcendentals=700_000),
        name="pair",
    )(*args, *consts)


def solution(mesh):
    placed = (
        P(None, "lat", "lon", None), P(), P(), P(), P("lat", None, None), P(), P(), P(), P("lat", None, None),
    )
    return jax.shard_map(
        shards, mesh=mesh, in_specs=placed, out_specs=P(None, "lat", "lon", None), check_vma=False
    )
```

time: 43.2 us -> 42 us (0.972)
  Pallas kernels: 41.4 us -> 40.2 us
    pallas_call x1, Pallas kernels: 41.4 us -> 40.2 us  [shards(): pl.pallas_call(functools.partial(kernel, nlat, nlon), out_shape=jax.Shape...]
where the time goes in v2:
time: 42 us; the launch traced here: 41.8 us
  Pallas kernels  40.2 us (96%)
  local copies, waits for them, and re-layouts  1.62 us (4%)
    pallas_call x1, Pallas kernels, shards(): pl.pallas_call(functools.partial(kernel, nlat, nlon), out_shape=jax.Shape...  40.2 us
    unnamed x1, local copies, waits for them, and re-layouts  1.62 us

profile of v2, /device:TPU:1, one launch (start us, length us, event | category | flops | bytes accessed | tf_op | source)
XLA Modules:
  0.0 41.8 jit_solution(131199001763736867)
XLA Ops:
  0.0 40.2 %pair.1 = bf16[1,12,12,512]{3,2,1,0:T(8,128)(2,1)} custom-call(bf16[1,12,12,512]{3,2,1,0:T(8,128)(2,1)} %tok_h.1, f32[1,512]{1,0:T(1,128)} %bitcast.2, bf16[512,1536]{1,0:T(8,128)(2,1)} %wqkv1_h.1, bf16[512,512]{1,0:T(8,128)(2,1)} %wproj1_h.1, f32[1,16,529]{2,1,0:T(8,128)} %bias1_h.1, f32[1,512]{1,0:T(1,128)} %bitcast.3, bf16[512,1536]{1,0:T(8,128)(2,1)} %wqkv2_h.1, ...), custom_call_target="tpu_custom_call" | custom-call | flops 2000000000 | bytes 8000000 | tf_op jit(solution)/shard_map/pair/pallas_call | solution.py:440
  40.2 1.6 %copy.22 = bf16[1,12,12,512]{3,2,1,0:T(8,128)(2,1)} copy(bf16[1,12,12,512]{3,2,1,0:T(8,128)(2,1)} %pair.1) | data formatting | bytes 294912

commit v3 on v2

--- a/solution.py
+++ b/solution.py
@@ -132,19 +132,18 @@
     return dot(order, parts)
 
 
-def attend(qhi, qlo, khi, klo, val, bias, size):
-    parts = []
-    ones = jnp.ones((val.shape[0], 128), BF16)
-    for g in range(4):
-        at = slice(128 * g, 128 * g + 128)
+def attend(windows, size):
+    units = [(w, slice(128 * g, 128 * g + 128), g) for w in windows for g in range(4)]
+    ones = jnp.ones((TOK, 128), BF16)
+    scores = []
+    for (qhi, qlo, khi, klo, _, bias), at, g in units:
         left = jnp.concatenate([qhi[:, at], qlo[:, at], qhi[:, at]], axis=1)
         right = jnp.concatenate([khi[:, at], khi[:, at], klo[:, at]], axis=1)
-        scores = dot_nt(left, right) + bias(g)
-        top = jnp.max(scores, axis=-1, keepdims=True)
-        expo = jnp.exp2(scores - top).astype(BF16)
-        both = dot(expo, jnp.concatenate([val[:, at], ones], axis=1))
-        parts.append(masked(both[:, :128] / both[:, 128:], size))
-    return jnp.concatenate(parts, axis=1)
+        scores.append(dot_nt(left, right) + bias(g))
+    expo = [jnp.exp2(x - jnp.max(x, axis=-1, keepdims=True)).astype(BF16) for x in scores]
+    both = [dot(e, jnp.concatenate([w[4][:, at], ones], axis=1)) for e, (w, at, _) in zip(expo, units)]
+    parts = [masked(x[:, :128] / x[:, 128:], size) for x in both]
+    return [jnp.concatenate(parts[4 * i : 4 * i + 4], axis=1) for i in range(len(windows))]
 
 
 def kernel(
@@ -221,8 +220,8 @@
     for name, _, _ in late_loads:
         loads[name].start()
     rep = const["rep"][...]
-    heads = attend(
-        masked(dot(rep, qhi), WIN), masked(dot(rep, qlo), WIN), khi, klo, val, lambda g: bias1[g], WIN
+    (heads,) = attend(
+        [(masked(dot(rep, qhi), WIN), masked(dot(rep, qlo), WIN), khi, klo, val, lambda g: bias1[g])], WIN
     )
     get("fold")
     get("wproj1")
@@ -326,15 +325,13 @@
         new = dot(dot(const["late"][...], new).astype(BF16), wqkv2[:, DIM:])
         for a in range(2):
             keyval[b, a, pl.ds(pl.multiple_of(72 * (1 - b), 8), 72), :] = new[72 * a : 72 * a + 72]
-        parts = []
+        windows = []
         for a in range(2):
             khi, klo = split(keyval[b, a, :, :DIM])
             val = keyval[b, a, :, DIM:].astype(BF16)
             at = pl.ds(TOK * a, TOK)
-            parts.append(
-                attend(ahi[b, at], alo[b, at], khi, klo, val, lambda g, a=a: bias2[a, b, g], HALF)
-            )
-        return dot(const["fold2"][b], jnp.concatenate(parts, axis=0))
+            windows.append((ahi[b, at], alo[b, at], khi, klo, val, lambda g, a=a: bias2[a, b, g]))
+        return dot(const["fold2"][b], jnp.concatenate(attend(windows, HALF), axis=0))
 
     unpack[...] = jnp.zeros_like(unpack)
     window_bias(1, tab2)

time: 42 us -> 38 us (0.905)
  Pallas kernels: 40.2 us -> 36.2 us
    pallas_call x1, Pallas kernels: 40.2 us -> 36.2 us  [shards(): pl.pallas_call(functools.partial(kernel, nlat, nlon), out_shape=jax.Shape...]
where the time goes in v3:
time: 38 us; the launch traced here: 37.9 us
  Pallas kernels  36.2 us (95%)
  local copies, waits for them, and re-layouts  1.62 us (4%)
    pallas_call x1, Pallas kernels, shards(): pl.pallas_call(functools.partial(kernel, nlat, nlon), out_shape=jax.Shape...  36.2 us
    unnamed x1, local copies, waits for them, and re-layouts  1.62 us

profile of v3, /device:TPU:1, one launch (start us, length us, event | category | flops | bytes accessed | tf_op | source)
XLA Modules:
  0.0 37.9 jit_solution(4698260957182783495)
XLA Ops:
  0.0 36.2 %pair.1 = bf16[1,12,12,512]{3,2,1,0:T(8,128)(2,1)} custom-call(bf16[1,12,12,512]{3,2,1,0:T(8,128)(2,1)} %tok_h.1, f32[1,512]{1,0:T(1,128)} %bitcast.2, bf16[512,1536]{1,0:T(8,128)(2,1)} %wqkv1_h.1, bf16[512,512]{1,0:T(8,128)(2,1)} %wproj1_h.1, f32[1,16,529]{2,1,0:T(8,128)} %bias1_h.1, f32[1,512]{1,0:T(1,128)} %bitcast.3, bf16[512,1536]{1,0:T(8,128)(2,1)} %wqkv2_h.1, ...), custom_call_target="tpu_custom_call" | custom-call | flops 2000000000 | bytes 8000000 | tf_op jit(solution)/shard_map/pair/pallas_call | solution.py:437
  36.2 1.6 %copy.22 = bf16[1,12,12,512]{3,2,1,0:T(8,128)(2,1)} copy(bf16[1,12,12,512]{3,2,1,0:T(8,128)(2,1)} %pair.1) | data formatting | bytes 294912

commit v4 on v3

--- a/solution.py
+++ b/solution.py
@@ -254,22 +254,9 @@
         peer = jnp.where(b == 0, west, east)
         return remote(packed.at[a, b], halo_lon.at[1 - b, a], lon_send.at[b, a], lon_recv.at[1 - b, a], (lat, peer))
 
-    for b in (side_far, side_near):
-        for a in (part0, 1 - part0):
-            edge(b, a).start()
+    edge(side_far, part0).start()
     to_n = remote(packed.at[0], halo_lat.at[1], lat_send.at[0], lat_recv.at[1], (north, lon))
     to_s = remote(packed.at[1], halo_lat.at[0], lat_send.at[1], lat_recv.at[0], (south, lon))
-
-    @pl.when(has_n)
-    def _():
-        to_n.start()
-
-    @pl.when(has_s)
-    def _():
-        to_s.start()
-
-    send_tab = remote(tab2, tabn, tab_send, tab_recv, (south, lon))
-    send_tab.start()
 
     for a, has in ((0, has_n), (1, has_s)):
         @pl.when(jnp.logical_not(has))
@@ -341,6 +328,20 @@
     rep = const["rep2"][...]
     ahi[...] = masked(dot(rep, qhi), HALF).reshape(2, 288, DIM)
     alo[...] = masked(dot(rep, qlo), HALF).reshape(2, 288, DIM)
+    edge(side_far, 1 - part0).start()
+    for a in (part0, 1 - part0):
+        edge(side_near, a).start()
+    @pl.when(has_n)
+    def _():
+        to_n.start()
+
+    @pl.when(has_s)
+    def _():
+        to_s.start()
+
+    send_tab = remote(tab2, tabn, tab_send, tab_recv, (south, lon))
+    send_tab.start()
+
     get("back")
     residual = dot(const["back"][...], first)
     get("early")

time: 38 us -> 37.8 us (level)
  no operation moved by 1% of the time
where the time goes in v4:
time: 37.8 us; the launch traced here: 37.7 us
  Pallas kernels  36 us (95%)
  local copies, waits for them, and re-layouts  1.62 us (4%)
    pallas_call x1, Pallas kernels, shards(): pl.pallas_call(functools.partial(kernel, nlat, nlon), out_shape=jax.Shape...  36 us
    unnamed x1, local copies, waits for them, and re-layouts  1.62 us

profile of v4, /device:TPU:1, one launch (start us, length us, event | category | flops | bytes accessed | tf_op | source)
XLA Modules:
  0.0 37.7 jit_solution(505901109827895354)
XLA Ops:
  0.0 36.0 %pair.1 = bf16[1,12,12,512]{3,2,1,0:T(8,128)(2,1)} custom-call(bf16[1,12,12,512]{3,2,1,0:T(8,128)(2,1)} %tok_h.1, f32[1,512]{1,0:T(1,128)} %bitcast.2, bf16[512,1536]{1,0:T(8,128)(2,1)} %wqkv1_h.1, bf16[512,512]{1,0:T(8,128)(2,1)} %wproj1_h.1, f32[1,16,529]{2,1,0:T(8,128)} %bias1_h.1, f32[1,512]{1,0:T(1,128)} %bitcast.3, bf16[512,1536]{1,0:T(8,128)(2,1)} %wqkv2_h.1, ...), custom_call_target="tpu_custom_call" | custom-call | flops 2000000000 | bytes 8000000 | tf_op jit(solution)/shard_map/pair/pallas_call | solution.py:438
  36.0 1.6 %copy.22 = bf16[1,12,12,512]{3,2,1,0:T(8,128)(2,1)} copy(bf16[1,12,12,512]{3,2,1,0:T(8,128)(2,1)} %pair.1) | data formatting | bytes 294912

commit v5 on v4

--- a/solution.py
+++ b/solution.py
@@ -254,6 +254,8 @@
         peer = jnp.where(b == 0, west, east)
         return remote(packed.at[a, b], halo_lon.at[1 - b, a], lon_send.at[b, a], lon_recv.at[1 - b, a], (lat, peer))
 
+    send_tab = remote(tab2, tabn, tab_send, tab_recv, (south, lon))
+    send_tab.start()
     edge(side_far, part0).start()
     to_n = remote(packed.at[0], halo_lat.at[1], lat_send.at[0], lat_recv.at[1], (north, lon))
     to_s = remote(packed.at[1], halo_lat.at[0], lat_send.at[1], lat_recv.at[0], (south, lon))
@@ -339,8 +341,6 @@
     def _():
         to_s.start()
 
-    send_tab = remote(tab2, tabn, tab_send, tab_recv, (south, lon))
-    send_tab.start()
 
     get("back")
     residual = dot(const["back"][...], first)

time: 37.8 us -> 37.8 us (level)
  no operation moved by 1% of the time
where the time goes in v5:
time: 37.8 us; the launch traced here: 37.7 us
  Pallas kernels  36.1 us (96%)
  local copies, waits for them, and re-layouts  1.62 us (4%)
    pallas_call x1, Pallas kernels, shards(): pl.pallas_call(functools.partial(kernel, nlat, nlon), out_shape=jax.Shape...  36.1 us
    unnamed x1, local copies, waits for them, and re-layouts  1.62 us

profile of v5, /device:TPU:1, one launch (start us, length us, event | category | flops | bytes accessed | tf_op | source)
XLA Modules:
  0.0 37.7 jit_solution(13513813747629143042)
XLA Ops:
  0.0 36.1 %pair.1 = bf16[1,12,12,512]{3,2,1,0:T(8,128)(2,1)} custom-call(bf16[1,12,12,512]{3,2,1,0:T(8,128)(2,1)} %tok_h.1, f32[1,512]{1,0:T(1,128)} %bitcast.2, bf16[512,1536]{1,0:T(8,128)(2,1)} %wqkv1_h.1, bf16[512,512]{1,0:T(8,128)(2,1)} %wproj1_h.1, f32[1,16,529]{2,1,0:T(8,128)} %bias1_h.1, f32[1,512]{1,0:T(1,128)} %bitcast.3, bf16[512,1536]{1,0:T(8,128)(2,1)} %wqkv2_h.1, ...), custom_call_target="tpu_custom_call" | custom-call | flops 2000000000 | bytes 8000000 | tf_op jit(solution)/shard_map/pair/pallas_call | solution.py:438
  36.1 1.6 %copy.22 = bf16[1,12,12,512]{3,2,1,0:T(8,128)(2,1)} copy(bf16[1,12,12,512]{3,2,1,0:T(8,128)(2,1)} %pair.1) | data formatting | bytes 294912
